TPU v7x, 512 devices: a whole 4x8x8 slice. The times are simulated.
512 devices in a mesh: dp: 16 (over y, core), rule: 32 (over x, z).
Axes of the slice: x: 4, y: 8, z: 8, core: 2. Of those that a mesh axis runs over, the one named last changes fastest.
Arguments:
- hidden_states: bfloat16 [4096, 8192], P(('dp', 'rule')), may hold values from -6 to 6
- attn_input: bfloat16 [4096, 8192], P(('dp', 'rule')), may hold values from -6 to 6
- rule_ids: int32 [4096, 2], replicated, may hold values from 0 to 127, as said below
- slot_ids: int32 [4096, 2], replicated, may hold values from -1 to 127, as said below
- cotangent: bfloat16 [4096, 2], replicated, may hold values from -6 to 6
- adapter_in: bfloat16 [128, 8192, 512], P('dp', 'rule'), may hold values from -0.0625 to 0.0625
- adapter_bias: float32 [128, 512], P('dp'), may hold values from -3 to 3
- adapter_out: float32 [128, 512], P('dp'), may hold values from -0.25 to 0.25
Outputs:
- rewards: bfloat16 [4096, 2], P('dp')
- adapter_in_grad: bfloat16 [128, 8192, 512], P('dp', 'rule')
- adapter_bias_grad: float32 [128, 512], P('dp')
- adapter_out_grad: float32 [128, 512], P('dp')
- o_proj_grad: bfloat16 [8192, 8192], P('rule', 'dp')
Inputs may be any that keep to these rules, and one draw needn't show every extreme that they name: `rule_ids`: the owner of rule r is r // 8. Among the 16 pairs of one block of 8 consecutive tokens at most 2 name rules of any one owner, and in every block some owner gets exactly 2. The two rules of a token differ. slot_ids[t, k] counts the earlier pairs, in the order of t then k, that name the same rule; it is -1 where that count reaches 128. Some rule fills all 128 rows.
All inputs are finite; a program needn't handle non-finite values.
Results may differ from a plain program's by a relative error of at most 0.03.
Values may be sent and summed in bfloat16 or wider, within the bound.
No kernel may reach another device: no remote copies, remote signals or barrier semaphores. Data moves between devices by JAX's collectives and lax.ppermute only.
A program may use at most 64 MiB of HBM per device.

v0:
```python
import jax
import jax.numpy as jnp
from jax import lax
from jax.sharding import PartitionSpec as P


def local(
    hidden_states, attn_input, rule_ids, slot_ids, cotangent, adapter_in, adapter_bias, adapter_out
):
    dp_size = lax.axis_size("dp")
    rule_size = lax.axis_size("rule")
    dp_index = lax.axis_index("dp")
    rule_index = lax.axis_index("rule")
    rows_dev = hidden_states.shape[0]
    adapters, feature_cols, hidden_units = adapter_in.shape
    send_cap = max(2, 4 * rows_dev // dp_size)
    capacity = 4 * rows_dev * rule_size // adapters
    block_count = dp_size * rule_size
    pair_count = 2 * rows_dev
    slot_count = dp_size * send_cap
    recv_count = slot_count * rule_size
    buffer_rows = adapters * capacity
    rule_all = rule_ids.reshape(block_count, pair_count)
    slot_all = slot_ids.reshape(block_count, pair_count)
    cot_all = cotangent.reshape(block_count, pair_count).astype(jnp.float32)
    owner_all = rule_all // adapters
    earlier = jnp.arange(pair_count)[None, :] < jnp.arange(pair_count)[:, None]
    same_owner = owner_all[:, :, None] == owner_all[:, None, :]
    rank_all = jnp.sum((same_owner & earlier[None]).astype(jnp.int32), axis=2)
    my_block = dp_index * rule_size + rule_index
    my_owner = lax.dynamic_index_in_dim(owner_all, my_block, 0, keepdims=False)
    my_rank = lax.dynamic_index_in_dim(rank_all, my_block, 0, keepdims=False)
    target = my_owner * send_cap + my_rank
    select_pairs = (jnp.arange(slot_count)[:, None] == target[None, :]).astype(jnp.int32)
    select_tokens = jnp.sum(select_pairs.reshape(slot_count, rows_dev, 2), axis=2).astype(
        jnp.bfloat16
    )
    outgoing = jnp.dot(select_tokens, hidden_states, preferred_element_type=jnp.float32).astype(
        jnp.bfloat16
    )
    outgoing = outgoing.reshape(dp_size, send_cap, rule_size, feature_cols)
    incoming = lax.all_to_all(
        lax.all_to_all(outgoing, "dp", split_axis=0, concat_axis=0, tiled=True),
        "rule",
        split_axis=2,
        concat_axis=2,
        tiled=True,
    )
    flat_in = jnp.concatenate(
        [incoming.reshape(recv_count, feature_cols), jnp.zeros((1, feature_cols), jnp.bfloat16)],
        axis=0,
    )
    block_dp = (jnp.arange(block_count) // rule_size)[:, None]
    block_rule = (jnp.arange(block_count) % rule_size)[:, None]
    recv_index = (block_dp * send_cap + rank_all) * rule_size + block_rule
    owned = (owner_all == dp_index) & (slot_all >= 0)
    buffer_pos = rule_all % adapters * capacity + slot_all
    pos_target = jnp.where(owned, buffer_pos, buffer_rows).reshape(-1)
    recv_target = jnp.where(owned, recv_index, recv_count).reshape(-1)
    to_recv = (
        jnp.full((buffer_rows + 1,), recv_count, jnp.int32)
        .at[pos_target]
        .set(recv_index.reshape(-1))[:buffer_rows]
    )
    to_buffer = (
        jnp.full((recv_count + 1,), buffer_rows, jnp.int32)
        .at[recv_target]
        .set(buffer_pos.reshape(-1))[:recv_count]
    )
    cot_buffer = (
        jnp.zeros((buffer_rows + 1,), jnp.float32)
        .at[pos_target]
        .set(cot_all.reshape(-1))[:buffer_rows]
    )
    cot_rows = cot_buffer.reshape(adapters, capacity)
    rows_buf = jnp.take(flat_in, to_recv, axis=0).reshape(adapters, capacity, feature_cols)
    partial_pre = jnp.einsum(
        "acd,adr->acr", rows_buf, adapter_in, preferred_element_type=jnp.float32
    )
    preact = (
        lax.psum(partial_pre.astype(jnp.bfloat16), "rule").astype(jnp.float32)
        + adapter_bias[:, None, :]
    )
    sigmoid_z = jax.nn.sigmoid(preact)
    activated = preact * sigmoid_z
    reward_rows = jnp.sum(activated * adapter_out[:, None, :], axis=2)
    grad_pre = (
        cot_rows[:, :, None]
        * adapter_out[:, None, :]
        * sigmoid_z
        * (1.0 + preact * (1.0 - sigmoid_z))
    )
    grad_half = grad_pre.astype(jnp.bfloat16)
    bias_grad = jnp.sum(grad_pre, axis=1)
    out_grad = jnp.sum(cot_rows[:, :, None] * activated, axis=1)
    reward_flat = jnp.concatenate([reward_rows.reshape(-1), jnp.zeros((1,), jnp.float32)]).astype(
        jnp.bfloat16
    )
    in_grad = jnp.einsum(
        "acd,acr->adr", rows_buf, grad_half, preferred_element_type=jnp.float32
    ).astype(jnp.bfloat16)
    input_grad = jnp.einsum(
        "acr,adr->acd", grad_half, adapter_in, preferred_element_type=jnp.float32
    ).astype(jnp.bfloat16)
    grad_flat = jnp.concatenate(
        [input_grad.reshape(buffer_rows, feature_cols), jnp.zeros((1, feature_cols), jnp.bfloat16)],
        axis=0,
    )
    back_rows = jnp.take(grad_flat, to_buffer, axis=0).reshape(
        dp_size, send_cap, rule_size, feature_cols
    )
    back_reward = jnp.take(reward_flat, to_buffer, axis=0).reshape(dp_size, send_cap, rule_size)
    returned, reward_back = (
        lax.all_to_all(back_rows, "dp", split_axis=0, concat_axis=0, tiled=True),
        lax.all_to_all(back_reward, "dp", split_axis=0, concat_axis=0, tiled=True),
    )
    owner_group = lax.dynamic_slice_in_dim(owner_all, dp_index * rule_size, rule_size, 0)
    rank_group = lax.dynamic_slice_in_dim(rank_all, dp_index * rule_size, rule_size, 0)
    pair_index = (
        (owner_group * send_cap + rank_group) * rule_size + jnp.arange(rule_size)[:, None]
    ).reshape(-1)
    pair_grads = jnp.take(returned.reshape(recv_count, feature_cols), pair_index, axis=0)
    pair_grads = pair_grads.astype(jnp.float32).reshape(rule_size * rows_dev, 2, feature_cols)
    state_grad = jnp.sum(pair_grads, axis=1).astype(jnp.bfloat16)
    rewards = jnp.take(reward_back.reshape(recv_count), pair_index, axis=0).reshape(
        rule_size * rows_dev, 2
    )
    group_term = lax.dot_general(
        state_grad,
        lax.all_gather(attn_input, "rule", axis=0, tiled=True),
        (((0,), (0,)), ((), ())),
        preferred_element_type=jnp.float32,
    )
    o_proj_grad = lax.psum_scatter(
        group_term.astype(jnp.bfloat16), "dp", scatter_dimension=1, tiled=True
    )
    return (rewards, in_grad, bias_grad, out_grad, o_proj_grad)


def solution(mesh):
    placed = (
        P(("dp", "rule"), None),
        P(("dp", "rule"), None),
        P(),
        P(),
        P(),
        P("dp", "rule", None),
        P("dp", None),
        P("dp", None),
    )
    return jax.shard_map(
        local,
        mesh=mesh,
        in_specs=placed,
        out_specs=(
            P("dp", None),
            P("dp", "rule", None),
            P("dp", None),
            P("dp", None),
            P("rule", "dp"),
        ),
        check_vma=False,
    )
```

profile of v0, /device:TPU:25, one launch (start us, length us, event | category | flops | bytes accessed | tf_op | source)
XLA Modules:
  0.0 413.3 jit_solution(5841563843183169320)
XLA Ops:
  7.2 2.9 copy.44
  10.1 2.2 reshape.437
  12.4 0.2 convert_reduce_fusion
  12.6 0.2 add_reduce_fusion
  13.0 0.3 convolution_convert_fusion.1
  13.5 1.3 copy.57
  14.8 9.4 %all-to-all-start = ((bf16[16,2,32,256]{3,1,2,0:T(2,128)(2,1)}), bf16[16,2,32,256]{3,1,2,0:T(2,128)(2,1)S(1)}, u32[]{:S(2)}, u32[]{:S(2)}) async-start(bf16[16,2,32,256]{3,1,2,0:T(2,128)(2,1)} %copy.57), calls=%async_computation | async-start | bytes 1048576 | tf_op jit(solution)/shard_map/all_to_all | solution.py:43
  24.3 3.0 reshape.439
  27.6 2.0 copy.51
  29.6 3.0 reshape.440
  32.7 0.2 compare_select_fusion.2
  32.9 6.3 %all-to-all-done = bf16[16,2,32,256]{3,1,2,0:T(2,128)(2,1)S(1)} async-done(((bf16[16,2,32,256]{3,1,2,0:T(2,128)(2,1)}), bf16[16,2,32,256]{3,1,2,0:T(2,128)(2,1)S(1)}, u32[]{:S(2)}, u32[]{:S(2)}) %all-to-all-start) | async-done | bytes 524320 | tf_op jit(solution)/shard_map/all_to_all | solution.py:43
  39.2 1.3 copy.58
  40.6 11.2 %all-to-all-start.1 = ((bf16[16,2,32,256]{3,1,0,2:T(2,128)(2,1)}), bf16[16,2,32,256]{3,1,0,2:T(2,128)(2,1)S(1)}, u32[]{:S(2)}, u32[]{:S(2)}) async-start(bf16[16,2,32,256]{3,1,0,2:T(2,128)(2,1)} %copy.58), calls=%async_computation.1 | async-start | bytes 1048576 | tf_op jit(solution)/shard_map/all_to_all | solution.py:42
  51.9 0.2 compare_select_fusion.1
  52.2 30.4 %scatter_custom_fusion.1 = s32[1025]{0:T(1024)S(1)} fusion(s32[8192]{0:T(1024)S(1)} %bitcast.35, s32[8192]{0:T(1024)S(1)} %reshape.505, s32[]{:T(128)} %constant.137.clone.1), kind=kCustom, calls=%fused_computation.76 | custom fusion | bytes 4104 | tf_op jit(solution)/shard_map/scatter | solution.py:63
  82.7 0.3 copy.59
  83.0 4.9 %gather_fusion.3 = bf16[1024,256]{1,0:T(8,128)(2,1)} fusion(bf16[1025,256]{1,0:T(8,128)(2,1)S(1)} %concatenate.10, s32[1024]{0:T(1024)S(1)} %fusion.23), kind=kCustom, calls=%fused_computation.clone | custom fusion | bytes 1052672 | tf_op jit(solution)/shard_map/jit(_take)/gather | solution.py:76
  88.0 1.2 broadcast_select_fusion.1
  89.2 1.5 convolution_convert_fusion.3
  90.7 0.2 all-gather.2.cloned.1.call-start
  90.9 0.5 all-gather.2.cloned.1.call-update
  91.5 2.7 reshape.441
  94.2 2.7 reshape.442
  97.0 30.4 %scatter_custom_fusion = s32[1025]{0:T(1024)S(1)} fusion(s32[8192]{0:T(1024)S(1)} %bitcast.34, s32[8192]{0:T(1024)S(1)} %fusion.7, s32[]{:T(128)} %constant.137.clone.1), kind=kCustom, calls=%fused_computation.78 | custom fusion | bytes 4104 | tf_op jit(solution)/shard_map/scatter | solution.py:68
  127.6 1.7 copy.61
  129.3 2.7 reshape.513
  132.0 30.4 %scatter_custom_fusion.2 = f32[1025]{0:T(1024)S(1)} fusion(s32[8192]{0:T(1024)S(1)} %bitcast.36, f32[8192]{0:T(1024)S(1)} %reshape.513, f32[]{:T(128)} %constant.147.clone.1), kind=kCustom, calls=%fused_computation.67 | custom fusion | bytes 4104 | tf_op jit(solution)/shard_map/scatter | solution.py:73
  162.5 83.6 %all-reduce.4.cloned.1.call-done = bf16[8,128,512]{2,1,0:T(8,128)(2,1)} async-done(((bf16[8,128,512]{2,1,0:T(8,128)(2,1)}), bf16[8,128,512]{2,1,0:T(8,128)(2,1)}) %all-reduce.4.cloned.1.call-update) | async-done | bytes 1048592 | tf_op jit(solution)/shard_map/psum | solution.py:81
  246.1 3.4 fusion.29
  249.5 6.8 %gather_fusion = bf16[1024]{0:T(1024)(128)(2,1)S(1)} fusion(bf16[1025]{0:T(1024)(128)(2,1)S(1)} %pad_maximum_fusion, s32[1024]{0:T(1024)S(1)} %get-tuple-element.34), kind=kCustom, calls=%fused_computation.2 | custom fusion | bytes 8192 | tf_op jit(solution)/shard_map/jit(_take)/gather | solution.py:112
  256.4 0.6 and_select_fusion.2
  257.0 12.1 %all-to-all-start.2 = ((bf16[16,2,32]{2,1,0:T(2,128)(2,1)}), bf16[16,2,32]{2,1,0:T(2,128)(2,1)S(1)}, u32[]{:S(2)}, u32[]{:S(2)}) async-start(bf16[16,2,32]{2,1,0:T(2,128)(2,1)} %and_select_fusion.2), calls=%async_computation.2 | async-start | bytes 16384 | tf_op jit(solution)/shard_map/all_to_all | solution.py:115
  269.1 2.3 convolution_convert_fusion.4
  271.5 5.0 %gather_fusion.4 = bf16[1024,256]{1,0:T(8,128)(2,1)} fusion(bf16[1025,256]{1,0:T(8,128)(2,1)S(1)} %concatenate.12, s32[1024]{0:T(1024)S(1)} %get-tuple-element.34), kind=kCustom, calls=%fused_computation.1.clone | custom fusion | bytes 1052672 | tf_op jit(solution)/shard_map/jit(_take)/gather | solution.py:109
  276.5 2.0 broadcast_select_fusion
  278.6 7.2 %all-to-all-start.3 = ((bf16[16,2,32,256]{3,2,1,0:T(8,128)(2,1)}), bf16[16,2,32,256]{3,2,1,0:T(8,128)(2,1)S(1)}, u32[]{:S(2)}, u32[]{:S(2)}) async-start(bf16[16,2,32,256]{3,2,1,0:T(8,128)(2,1)} %bitcast.29), calls=%async_computation.3 | async-start | bytes 1048576 | tf_op jit(solution)/shard_map/all_to_all | solution.py:114
  285.8 0.3 reduce-scatter.2.cloned.1.call-start
  286.5 3.5 gather_fusion.1
  290.0 0.2 gather.24
  290.3 10.5 %all-to-all-done.3 = bf16[16,2,32,256]{3,2,1,0:T(8,128)(2,1)S(1)} async-done(((bf16[16,2,32,256]{3,2,1,0:T(8,128)(2,1)}), bf16[16,2,32,256]{3,2,1,0:T(8,128)(2,1)S(1)}, u32[]{:S(2)}, u32[]{:S(2)}) %all-to-all-start.3) | async-done | bytes 524320 | tf_op jit(solution)/shard_map/all_to_all | solution.py:114
  300.8 1.9 gather_fusion.2
  302.8 2.0 fusion.3
  304.8 31.3 %all-gather.2.cloned.1.call-done = bf16[256,8192]{1,0:T(8,128)(2,1)} async-done(((bf16[8,8192]{1,0:T(8,128)(2,1)}), bf16[256,8192]{1,0:T(8,128)(2,1)}) %all-gather.2.cloned.1.call-update) | async-done | bytes 4194320 | tf_op jit(solution)/shard_map/all_gather | solution.py:130
  336.2 5.4 %convolution_convert_fusion = bf16[256,8192]{1,0:T(8,128)(2,1)} fusion(bf16[256,256]{1,0:T(8,128)(2,1)S(1)} %fusion.3, bf16[256,8192]{1,0:T(8,128)(2,1)} %all-gather.2.cloned.1.call-done), kind=kOutput, calls=%fused_computation.8 | convolution fusion | flops 1075838976 | bytes 8519680 | tf_op jit(solution)/shard_map/dot_general | solution.py:128
  341.6 3.8 convolution_convert_fusion.2
  345.4 0.7 copy.63
  346.1 60.7 %reduce-scatter.2.cloned.1.call-done = bf16[256,512]{1,0:T(8,128)(2,1)} async-done(((bf16[256,8192]{1,0:T(8,128)(2,1)}), bf16[256,512]{1,0:T(8,128)(2,1)}) %reduce-scatter.2.cloned.1.call-update) | async-done | bytes 262160 | tf_op jit(solution)/shard_map/reduce_scatter | solution.py:134
  (49 shorter events, 1.9 us)
Async XLA Ops:
  7.2 82.1 %copy-start = (bf16[8,256,512]{2,1,0:T(8,128)(2,1)S(1)}, bf16[8,256,512]{2,1,0:T(8,128)(2,1)}, u32[]{:S(2)}) copy-start(bf16[8,256,512]{2,1,0:T(8,128)(2,1)} %param.15) | copy-start | bytes 6291460
  7.2 5.8 %copy-start.1 = (bf16[8,8192]{1,0:T(8,128)(2,1)S(1)}, bf16[8,8192]{1,0:T(8,128)(2,1)}, u32[]{:S(2)}) copy-start(bf16[8,8192]{1,0:T(8,128)(2,1)} %param.10) | copy-start | bytes 393220
  14.8 12.8 %copy-start.2 = (s32[4096,2]{0,1:T(2,128)S(1)}, s32[4096,2]{0,1:T(2,128)}, u32[]{:S(2)}) copy-start(s32[4096,2]{0,1:T(2,128)} %param.13) | copy-start | bytes 98308
  14.8 24.4 %all-to-all-start = ((bf16[16,2,32,256]{3,1,2,0:T(2,128)(2,1)}), bf16[16,2,32,256]{3,1,2,0:T(2,128)(2,1)S(1)}, u32[]{:S(2)}, u32[]{:S(2)}) async-start(bf16[16,2,32,256]{3,1,2,0:T(2,128)(2,1)} %copy.57), calls=%async_computation | async-start | bytes 1048576 | tf_op jit(solution)/shard_map/all_to_all | solution.py:43
  40.6 42.1 %all-to-all-start.1 = ((bf16[16,2,32,256]{3,1,0,2:T(2,128)(2,1)}), bf16[16,2,32,256]{3,1,0,2:T(2,128)(2,1)S(1)}, u32[]{:S(2)}, u32[]{:S(2)}) async-start(bf16[16,2,32,256]{3,1,0,2:T(2,128)(2,1)} %copy.58), calls=%async_computation.1 | async-start | bytes 1048576 | tf_op jit(solution)/shard_map/all_to_all | solution.py:42
  51.8 194.3 %all-reduce.4.cloned.1.call-start = ((), (), s32[]{:S(2)}) async-start(), calls=%async_computation.5 | async-start | bytes 2097152 | tf_op jit(solution)/shard_map/psum | solution.py:81
  90.7 245.4 %all-gather.2.cloned.1.call-start = ((), (), s32[]{:S(2)}) async-start(), calls=%async_computation.6 | async-start | bytes 4325376 | tf_op jit(solution)/shard_map/all_gather | solution.py:130
  91.5 36.1 %copy-start.3 = (bf16[4096,2]{0,1:T(2,128)(2,1)S(1)}, bf16[4096,2]{0,1:T(2,128)(2,1)}, u32[]{:S(2)}) copy-start(bf16[4096,2]{0,1:T(2,128)(2,1)} %param.14) | copy-start | bytes 49156
  127.5 118.6 %copy-start.4 = (f32[8,512]{1,0:T(8,128)S(1)}, f32[8,512]{1,0:T(8,128)}, u32[]{:S(2)}) copy-start(f32[8,512]{1,0:T(8,128)} %param.16) | copy-start | bytes 49156
  127.5 118.6 %copy-start.5 = (f32[8,512]{1,0:T(8,128)S(1)}, f32[8,512]{1,0:T(8,128)}, u32[]{:S(2)}) copy-start(f32[8,512]{1,0:T(8,128)} %param.17) | copy-start | bytes 49156
  257.0 21.5 %all-to-all-start.2 = ((bf16[16,2,32]{2,1,0:T(2,128)(2,1)}), bf16[16,2,32]{2,1,0:T(2,128)(2,1)S(1)}, u32[]{:S(2)}, u32[]{:S(2)}) async-start(bf16[16,2,32]{2,1,0:T(2,128)(2,1)} %and_select_fusion.2), calls=%async_computation.2 | async-start | bytes 16384 | tf_op jit(solution)/shard_map/all_to_all | solution.py:115
  278.6 22.2 %all-to-all-start.3 = ((bf16[16,2,32,256]{3,2,1,0:T(8,128)(2,1)}), bf16[16,2,32,256]{3,2,1,0:T(8,128)(2,1)S(1)}, u32[]{:S(2)}, u32[]{:S(2)}) async-start(bf16[16,2,32,256]{3,2,1,0:T(8,128)(2,1)} %bitcast.29), calls=%async_computation.3 | async-start | bytes 1048576 | tf_op jit(solution)/shard_map/all_to_all | solution.py:114
  285.8 121.0 %reduce-scatter.2.cloned.1.call-start = ((), (), s32[]{:S(2)}) async-start(), calls=%async_computation.7 | async-start | bytes 4456448 | tf_op jit(solution)/shard_map/reduce_scatter | solution.py:134
Sparse Core Ops, SparseCore 0:
  90.8 155.2 all-reduce.3
  249.3 86.8 all-gather.1
  341.7 65.0 reduce-scatter.1
where the time goes:
time: 414 us; the launch traced here: 413 us
  waiting for transfers between devices  193 us (47%)
  local copies, waits for them, and re-layouts  142 us (34%)
  starting transfers between devices  40.5 us (10%)
  between operations  14.1 us (3%)
  matrix products  13.4 us (3%)
  other arithmetic  10.4 us (3%)
    psum x1, waiting for transfers between devices, local(): lax.psum(partial_pre.astype(jnp.bfloat16), 'rule').astype(jnp.float32)  83.6 us
    reduce_scatter x1, waiting for transfers between devices, local(): lax.psum_scatter(group_term.astype(jnp.bfloat16), 'dp', scatter_dimension...  60.7 us
    all_gather x1, waiting for transfers between devices, local(): lax.all_gather(attn_input, 'rule', axis=0, tiled=True)  31.3 us
    scatter x1, local copies, waits for them, and re-layouts, local(): to_recv = jnp.full((buffer_rows + 1,), recv_count, jnp.int32).at[pos_targ...  30.4 us
    scatter x1, local copies, waits for them, and re-layouts, local(): to_buffer = jnp.full((recv_count + 1,), buffer_rows, jnp.int32).at[recv_t...  30.4 us
    scatter x1, local copies, waits for them, and re-layouts, local(): cot_buffer = jnp.zeros((buffer_rows + 1,), jnp.float32).at[pos_target].se...  30.4 us
    all_to_all x1, starting transfers between devices, local(): lax.all_to_all(back_reward, 'dp', split_axis=0, concat_axis=0, tiled=True)  12.1 us
    all_to_all x1, starting transfers between devices, local(): lax.all_to_all(lax.all_to_all(outgoing, 'dp', split_axis=0, concat_axis=0...  11.2 us
  transfers between devices with their start and end apart: 7, of which 5 were waited for; matrix products, arithmetic and copies ran while one was open for 35% of the time, Pallas kernels for 0%

commit v1 on v0

--- a/solution.py
+++ b/solution.py
@@ -78,7 +78,9 @@
         "acd,adr->acr", rows_buf, adapter_in, preferred_element_type=jnp.float32
     )
     preact = (
-        lax.psum(partial_pre.astype(jnp.bfloat16), "rule").astype(jnp.float32)
+        jnp.sum(lax.all_gather(partial_pre.astype(jnp.bfloat16), "rule"), axis=0).astype(
+            jnp.float32
+        )
         + adapter_bias[:, None, :]
     )
     sigmoid_z = jax.nn.sigmoid(preact)

time: 414 us -> 491 us (1.19)
  waiting for transfers between devices: 193 us -> 267 us
  other arithmetic: 10.4 us -> 19.7 us
    all_gather x0 -> x1, waiting for transfers between devices: none -> 166 us  [local(): lax.all_gather(partial_pre.astype(jnp.bfloat16), 'rule')]
    psum x1 -> x0, waiting for transfers between devices: 83.6 us -> none  [local(): lax.psum(partial_pre.astype(jnp.bfloat16), 'rule').astype(jnp.float32)]
    all_gather x1, waiting for transfers between devices: 31.3 us -> 19.6 us  [local(): lax.all_gather(attn_input, 'rule', axis=0, tiled=True)]
    reduce_sum x0 -> x1, other arithmetic: none -> 11.4 us  [local(): jnp.sum(lax.all_gather(partial_pre.astype(jnp.bfloat16), 'rule'), axis=0)]
  transfers between devices with their start and end apart: 7 -> 7, of which waited for: 5 -> 6; matrix products, arithmetic and copies ran while one was open for 35% -> 31% of each run, Pallas kernels for 0% -> 0%
where the time goes in v1:
time: 491 us; the launch traced here: 490 us
  waiting for transfers between devices  267 us (54%)
  local copies, waits for them, and re-layouts  142 us (29%)
  starting transfers between devices  35.8 us (7%)
  other arithmetic  19.7 us (4%)
  between operations  14.2 us (3%)
  matrix products  11.9 us (2%)
    all_gather x1, waiting for transfers between devices, local(): lax.all_gather(partial_pre.astype(jnp.bfloat16), 'rule')  166 us
    reduce_scatter x1, waiting for transfers between devices, local(): lax.psum_scatter(group_term.astype(jnp.bfloat16), 'dp', scatter_dimension...  59.7 us
    scatter x1, local copies, waits for them, and re-layouts, local(): to_recv = jnp.full((buffer_rows + 1,), recv_count, jnp.int32).at[pos_targ...  30.4 us
    scatter x1, local copies, waits for them, and re-layouts, local(): to_buffer = jnp.full((recv_count + 1,), buffer_rows, jnp.int32).at[recv_t...  30.4 us
    scatter x1, local copies, waits for them, and re-layouts, local(): cot_buffer = jnp.zeros((buffer_rows + 1,), jnp.float32).at[pos_target].se...  30.4 us
    all_gather x1, waiting for transfers between devices, local(): lax.all_gather(attn_input, 'rule', axis=0, tiled=True)  19.6 us
    reduce_sum x1, other arithmetic, local(): jnp.sum(lax.all_gather(partial_pre.astype(jnp.bfloat16), 'rule'), axis=0)  11.4 us
    all_to_all x1, starting transfers between devices, local(): lax.all_to_all(lax.all_to_all(outgoing, 'dp', split_axis=0, concat_axis=0...  11.2 us
  transfers between devices with their start and end apart: 7, of which 6 were waited for; matrix products, arithmetic and copies ran while one was open for 31% of the time, Pallas kernels for 0%

profile of v1, /device:TPU:25, one launch (start us, length us, event | category | flops | bytes accessed | tf_op | source)
XLA Modules:
  0.0 490.1 jit_solution(9637768356110151887)
XLA Ops:
  7.2 2.9 copy.44
  10.1 2.2 reshape.437
  13.0 0.3 convolution_convert_fusion.1
  13.5 1.3 copy.57
  14.8 9.4 %all-to-all-start = ((bf16[16,2,32,256]{3,1,2,0:T(2,128)(2,1)}), bf16[16,2,32,256]{3,1,2,0:T(2,128)(2,1)S(1)}, u32[]{:S(2)}, u32[]{:S(2)}) async-start(bf16[16,2,32,256]{3,1,2,0:T(2,128)(2,1)} %copy.57), calls=%async_computation | async-start | bytes 1048576 | tf_op jit(solution)/shard_map/all_to_all | solution.py:43
  24.3 3.0 reshape.439
  27.6 2.0 copy.51
  29.6 3.0 reshape.440
  32.6 0.2 compare_select_fusion.2
  32.9 6.4 %all-to-all-done = bf16[16,2,32,256]{3,1,2,0:T(2,128)(2,1)S(1)} async-done(((bf16[16,2,32,256]{3,1,2,0:T(2,128)(2,1)}), bf16[16,2,32,256]{3,1,2,0:T(2,128)(2,1)S(1)}, u32[]{:S(2)}, u32[]{:S(2)}) %all-to-all-start) | async-done | bytes 524320 | tf_op jit(solution)/shard_map/all_to_all | solution.py:43
  39.2 1.3 copy.58
  40.6 11.2 %all-to-all-start.1 = ((bf16[16,2,32,256]{3,1,0,2:T(2,128)(2,1)}), bf16[16,2,32,256]{3,1,0,2:T(2,128)(2,1)S(1)}, u32[]{:S(2)}, u32[]{:S(2)}) async-start(bf16[16,2,32,256]{3,1,0,2:T(2,128)(2,1)} %copy.58), calls=%async_computation.1 | async-start | bytes 1048576 | tf_op jit(solution)/shard_map/all_to_all | solution.py:42
  52.2 30.4 %scatter_custom_fusion.1 = s32[1025]{0:T(1024)S(1)} fusion(s32[8192]{0:T(1024)S(1)} %bitcast.33, s32[8192]{0:T(1024)S(1)} %reshape.505, s32[]{:T(128)} %constant.138.clone.1), kind=kCustom, calls=%fused_computation.76 | custom fusion | bytes 4104 | tf_op jit(solution)/shard_map/scatter | solution.py:63
  82.7 0.3 copy.59
  83.0 3.9 gather_fusion.3
  87.0 0.2 broadcast_select_fusion.1
  87.2 0.8 copy-done.3
  88.0 1.5 convolution_convert_fusion.3
  89.4 0.2 all-gather.4.cloned.1.call-start
  89.7 0.5 all-gather.4.cloned.1.call-update
  90.2 2.7 reshape.441
  93.0 2.7 reshape.442
  95.7 1.7 copy.61
  97.4 2.7 reshape.513
  100.2 30.4 %scatter_custom_fusion = s32[1025]{0:T(1024)S(1)} fusion(s32[8192]{0:T(1024)S(1)} %bitcast.32, s32[8192]{0:T(1024)S(1)} %fusion.7, s32[]{:T(128)} %constant.138.clone.1), kind=kCustom, calls=%fused_computation.78 | custom fusion | bytes 4104 | tf_op jit(solution)/shard_map/scatter | solution.py:68
  130.7 30.4 %scatter_custom_fusion.2 = f32[1025]{0:T(1024)S(1)} fusion(s32[8192]{0:T(1024)S(1)} %bitcast.34, f32[8192]{0:T(1024)S(1)} %reshape.513, f32[]{:T(128)} %constant.148.clone.1), kind=kCustom, calls=%fused_computation.67 | custom fusion | bytes 4104 | tf_op jit(solution)/shard_map/scatter | solution.py:73
  161.2 166.5 %all-gather.6.cloned.1.call-done = bf16[256,128,512]{2,1,0:T(8,128)(2,1)} async-done(((bf16[8,128,512]{2,1,0:T(8,128)(2,1)}), bf16[256,128,512]{2,1,0:T(8,128)(2,1)}) %all-gather.6.cloned.1.call-update) | async-done | bytes 33554448 | tf_op jit(solution)/shard_map/all_gather | solution.py:81
  327.7 11.4 %reduce_sum.71 = bf16[8,128,512]{2,1,0:T(8,128)(2,1)S(1)} reduce(bf16[32,8,128,512]{3,2,1,0:T(8,128)(2,1)} %bitcast.24, bf16[]{:T(256)} %constant.146.clone.1), dimensions={0}, to_apply=%region_4.6 | reduce | flops 16252928 | bytes 34603008 | tf_op jit(solution)/shard_map/reduce_sum | solution.py:81
  339.2 1.1 convolution_convert_fusion.4
  340.3 3.9 gather_fusion.4
  344.3 3.4 fusion.29
  347.7 6.8 %gather_fusion = bf16[1024]{0:T(1024)(128)(2,1)S(1)} fusion(bf16[1025]{0:T(1024)(128)(2,1)S(1)} %pad_maximum_fusion, s32[1024]{0:T(1024)S(1)} %get-tuple-element.34), kind=kCustom, calls=%fused_computation.2 | custom fusion | bytes 8192 | tf_op jit(solution)/shard_map/jit(_take)/gather | solution.py:114
  354.6 0.6 and_select_fusion.2
  355.2 7.9 %all-to-all-start.2 = ((bf16[16,2,32]{2,1,0:T(2,128)(2,1)}), bf16[16,2,32]{2,1,0:T(2,128)(2,1)S(1)}, u32[]{:S(2)}, u32[]{:S(2)}) async-start(bf16[16,2,32]{2,1,0:T(2,128)(2,1)} %and_select_fusion.2), calls=%async_computation.2 | async-start | bytes 16384 | tf_op jit(solution)/shard_map/all_to_all | solution.py:117
  363.1 1.0 broadcast_select_fusion
  364.1 3.3 all-to-all-done.2
  367.4 6.7 %all-to-all-start.3 = ((bf16[16,2,32,256]{3,2,1,0:T(8,128)(2,1)}), bf16[16,2,32,256]{3,2,1,0:T(8,128)(2,1)S(1)}, u32[]{:S(2)}, u32[]{:S(2)}) async-start(bf16[16,2,32,256]{3,2,1,0:T(8,128)(2,1)} %bitcast.9), calls=%async_computation.3 | async-start | bytes 1048576 | tf_op jit(solution)/shard_map/all_to_all | solution.py:116
  374.1 0.3 reduce-scatter.2.cloned.1.call-start
  374.8 3.5 gather_fusion.1
  378.6 10.7 %all-to-all-done.3 = bf16[16,2,32,256]{3,2,1,0:T(8,128)(2,1)S(1)} async-done(((bf16[16,2,32,256]{3,2,1,0:T(8,128)(2,1)}), bf16[16,2,32,256]{3,2,1,0:T(8,128)(2,1)S(1)}, u32[]{:S(2)}, u32[]{:S(2)}) %all-to-all-start.3) | async-done | bytes 524320 | tf_op jit(solution)/shard_map/all_to_all | solution.py:116
  389.3 1.9 gather_fusion.2
  391.4 2.0 fusion.3
  393.4 19.6 %all-gather.4.cloned.1.call-done = bf16[256,8192]{1,0:T(8,128)(2,1)} async-done(((bf16[8,8192]{1,0:T(8,128)(2,1)}), bf16[256,8192]{1,0:T(8,128)(2,1)}) %all-gather.4.cloned.1.call-update) | async-done | bytes 4194320 | tf_op jit(solution)/shard_map/all_gather | solution.py:132
  412.9 5.4 %convolution_convert_fusion = bf16[256,8192]{1,0:T(8,128)(2,1)} fusion(bf16[256,256]{1,0:T(8,128)(2,1)S(1)} %fusion.3, bf16[256,8192]{1,0:T(8,128)(2,1)} %all-gather.4.cloned.1.call-done), kind=kOutput, calls=%fused_computation.8 | convolution fusion | flops 1075838976 | bytes 8519680 | tf_op jit(solution)/shard_map/dot_general | solution.py:130
  418.4 1.2 copy-done.2
  419.6 3.6 convolution_convert_fusion.2
  423.2 0.7 copy.63
  423.8 59.7 %reduce-scatter.2.cloned.1.call-done = bf16[256,512]{1,0:T(8,128)(2,1)} async-done(((bf16[256,8192]{1,0:T(8,128)(2,1)}), bf16[256,512]{1,0:T(8,128)(2,1)}) %reduce-scatter.2.cloned.1.call-update) | async-done | bytes 262160 | tf_op jit(solution)/shard_map/reduce_scatter | solution.py:136
  (56 shorter events, 2.6 us)
Async XLA Ops:
  7.2 80.8 %copy-start = (bf16[8,256,512]{2,1,0:T(8,128)(2,1)S(1)}, bf16[8,256,512]{2,1,0:T(8,128)(2,1)}, u32[]{:S(2)}) copy-start(bf16[8,256,512]{2,1,0:T(8,128)(2,1)} %param.15) | copy-start | bytes 6291460
  7.2 5.8 %copy-start.4 = (bf16[8,8192]{1,0:T(8,128)(2,1)S(1)}, bf16[8,8192]{1,0:T(8,128)(2,1)}, u32[]{:S(2)}) copy-start(bf16[8,8192]{1,0:T(8,128)(2,1)} %param.10) | copy-start | bytes 393220
  14.8 12.8 %copy-start.5 = (s32[4096,2]{0,1:T(2,128)S(1)}, s32[4096,2]{0,1:T(2,128)}, u32[]{:S(2)}) copy-start(s32[4096,2]{0,1:T(2,128)} %param.13) | copy-start | bytes 98308
  14.8 24.4 %all-to-all-start = ((bf16[16,2,32,256]{3,1,2,0:T(2,128)(2,1)}), bf16[16,2,32,256]{3,1,2,0:T(2,128)(2,1)S(1)}, u32[]{:S(2)}, u32[]{:S(2)}) async-start(bf16[16,2,32,256]{3,1,2,0:T(2,128)(2,1)} %copy.57), calls=%async_computation | async-start | bytes 1048576 | tf_op jit(solution)/shard_map/all_to_all | solution.py:43
  40.6 42.1 %all-to-all-start.1 = ((bf16[16,2,32,256]{3,1,0,2:T(2,128)(2,1)}), bf16[16,2,32,256]{3,1,0,2:T(2,128)(2,1)S(1)}, u32[]{:S(2)}, u32[]{:S(2)}) async-start(bf16[16,2,32,256]{3,1,0,2:T(2,128)(2,1)} %copy.58), calls=%async_computation.1 | async-start | bytes 1048576 | tf_op jit(solution)/shard_map/all_to_all | solution.py:42
  51.8 275.9 %all-gather.6.cloned.1.call-start = ((), (), s32[]{:S(2)}) async-start(), calls=%async_computation.7 | async-start | bytes 34603008 | tf_op jit(solution)/shard_map/all_gather | solution.py:81
  87.2 0.8 copy-start.3
  89.4 323.5 %all-gather.4.cloned.1.call-start = ((), (), s32[]{:S(2)}) async-start(), calls=%async_computation.5 | async-start | bytes 4325376 | tf_op jit(solution)/shard_map/all_gather | solution.py:132
  90.2 5.5 %copy-start.6 = (bf16[4096,2]{0,1:T(2,128)(2,1)S(1)}, bf16[4096,2]{0,1:T(2,128)(2,1)}, u32[]{:S(2)}) copy-start(bf16[4096,2]{0,1:T(2,128)(2,1)} %param.14) | copy-start | bytes 49156
  327.7 11.4 %copy-start.7 = (f32[8,512]{1,0:T(8,128)S(1)}, f32[8,512]{1,0:T(8,128)}, u32[]{:S(2)}) copy-start(f32[8,512]{1,0:T(8,128)} %param.16) | copy-start | bytes 49156
  327.7 11.4 %copy-start.8 = (f32[8,512]{1,0:T(8,128)S(1)}, f32[8,512]{1,0:T(8,128)}, u32[]{:S(2)}) copy-start(f32[8,512]{1,0:T(8,128)} %param.17) | copy-start | bytes 49156
  339.2 1.1 copy-start.1
  355.2 12.2 %all-to-all-start.2 = ((bf16[16,2,32]{2,1,0:T(2,128)(2,1)}), bf16[16,2,32]{2,1,0:T(2,128)(2,1)S(1)}, u32[]{:S(2)}, u32[]{:S(2)}) async-start(bf16[16,2,32]{2,1,0:T(2,128)(2,1)} %and_select_fusion.2), calls=%async_computation.2 | async-start | bytes 16384 | tf_op jit(solution)/shard_map/all_to_all | solution.py:117
  367.4 21.9 %all-to-all-start.3 = ((bf16[16,2,32,256]{3,2,1,0:T(8,128)(2,1)}), bf16[16,2,32,256]{3,2,1,0:T(8,128)(2,1)S(1)}, u32[]{:S(2)}, u32[]{:S(2)}) async-start(bf16[16,2,32,256]{3,2,1,0:T(8,128)(2,1)} %bitcast.9), calls=%async_computation.3 | async-start | bytes 1048576 | tf_op jit(solution)/shard_map/all_to_all | solution.py:116
  374.1 109.4 %reduce-scatter.2.cloned.1.call-start = ((), (), s32[]{:S(2)}) async-start(), calls=%async_computation.6 | async-start | bytes 4456448 | tf_op jit(solution)/shard_map/reduce_scatter | solution.py:136
  418.3 1.2 copy-start.2
Sparse Core Ops, SparseCore 0:
  89.6 238.0 all-gather.5
  330.9 82.0 all-gather.3
  418.5 65.0 reduce-scatter.1
